TPU v7x, 128 devices: a whole 4x4x4 slice. The times are simulated.
128 devices in a mesh: row: 8 (over x_lo, y), col: 16 (over x_hi, z, core).
Axes of the slice: x: 4 (x_hi: 2, x_lo: 2; x = x_hi * 2 + x_lo), y: 4, z: 4, core: 2. Of those that a mesh axis runs over, the one named last changes fastest.
Arguments:
- inverse: bfloat16 [26624, 26624], P('row', 'col'), may hold values from -6 to 6
- panels: bfloat16 [2, 8192, 512], P(None, 'col'), may hold values from -0.0625 to 0.0625
- block_slot: int32 [208], replicated, may hold values from 0 to 207, as said below
- list_ids: int32 [2, 64], replicated, may hold values from 0 to 207, as said below
Outputs:
- packed_panels: float32 [2, 16384, 512], P(None, ('row', 'col'))
- diag_update: float32 [2, 512, 512], replicated
Inputs may be any that keep to these rules, and one draw needn't show every extreme that they name: block_slot is a permutation of the slots. `list_ids`: each supernode lists distinct blocks; at most 16 of a supernode's listed blocks have slots in one grid row (slot // 26 equal), and in every supernode some grid row holds exactly 16. `list_ids`: in each aligned group of 4 list positions of a supernode, at most 1 listed blocks have slots in one grid column (slot // 13 equal).
All inputs are finite; a program needn't handle non-finite values.
Results may differ from a plain program's by a relative error of at most 0.0003.
Values may be sent and summed in bfloat16 or wider, within the bound.
A program may use at most 128 MiB of HBM per device.

v0:
```python
import jax
import jax.numpy as jnp
from jax import lax
from jax.sharding import PartitionSpec as P

BS = 128


def split_up(array, dim, devices):
    dims = array.shape
    pieces = array.reshape(*dims[:dim], devices, dims[dim] // devices, *dims[dim + 1 :])
    return jnp.moveaxis(pieces, dim, 0)


def sent_and_summed(array, axis, dim):
    pieces = split_up(array, dim, lax.axis_size(axis))
    arrived = lax.all_to_all(pieces, axis, split_axis=0, concat_axis=0, tiled=True)
    return arrived.astype(jnp.float32).sum(axis=0)


def lookup_slots(block_slot, list_ids):
    block_ids = jnp.arange(block_slot.shape[0], dtype=jnp.int32)
    matches = list_ids[..., None] == block_ids
    return jnp.sum(jnp.where(matches, block_slot, 0), axis=-1)


def exact_product(left_rows, right_rows):
    return jnp.dot(left_rows.astype(jnp.float32).T, right_rows, precision=lax.Precision.HIGHEST)


def local(inverse, panels, block_slot, list_ids):
    panel_width = panels.shape[2]
    row_blocks = inverse.shape[0] // BS
    col_blocks = inverse.shape[1] // BS
    listed = list_ids.shape[1]
    grid_rows = lax.axis_size("row")
    grid_cols = lax.axis_size("col")
    max_rows = 2 * listed // grid_rows
    own_rows = max_rows * BS // grid_cols
    shard_len = panels.shape[1] // BS
    slot_cap = (col_blocks + grid_cols - 1) // grid_cols
    my_row = lax.axis_index("row")
    my_col = lax.axis_index("col")
    slots = lookup_slots(block_slot, list_ids)
    grid_row = slots // row_blocks
    local_row = slots % row_blocks
    grid_col = slots // col_blocks
    local_col = slots % col_blocks
    a_blocks = inverse.reshape(row_blocks, BS, col_blocks * BS)
    positions = jnp.arange(listed, dtype=jnp.int32)
    col_ids = jnp.arange(col_blocks, dtype=jnp.int32)
    shard_of = positions // shard_len
    local_pos = my_col * shard_len + jnp.arange(shard_len, dtype=jnp.int32)
    panel_sums = []
    diag_terms = []
    for supernode in range(panels.shape[0]):
        cols_here = grid_col[supernode]
        in_row = grid_row[supernode] == my_row
        chosen_pos = jnp.argsort(jnp.where(in_row, positions, listed + positions), stable=True)[
            :max_rows
        ]
        is_valid = in_row[chosen_pos]
        picked = a_blocks[local_row[supernode][chosen_pos]]
        picked = jnp.where(is_valid[:, None, None], picked, jnp.zeros((), jnp.bfloat16)).reshape(
            max_rows * BS, col_blocks * BS
        )
        local_blocks = panels[supernode].reshape(shard_len, BS, panel_width)
        same_group = (
            (cols_here[:, None] == cols_here[None, :])
            & (shard_of[:, None] == shard_of[None, :])
            & (positions[None, :] < positions[:, None])
        )
        same_rank = jnp.sum(same_group.astype(jnp.int32), axis=1)
        dest_ids = jnp.arange(grid_cols * slot_cap, dtype=jnp.int32)
        send_pick = (
            (cols_here[local_pos] * slot_cap + same_rank[local_pos])[None, :] == dest_ids[:, None]
        ).astype(jnp.bfloat16)
        outgoing = jnp.einsum(
            "mj,jbw->mbw", send_pick, local_blocks, preferred_element_type=jnp.float32
        )
        outgoing = outgoing.astype(jnp.bfloat16).reshape(grid_cols * slot_cap * BS, panel_width)
        incoming = lax.all_to_all(outgoing, "col", split_axis=0, concat_axis=0, tiled=True)
        incoming = incoming.reshape(grid_cols * slot_cap, BS, panel_width)
        mine_here = cols_here == my_col
        to_column = (
            mine_here[:, None] & (local_col[supernode][:, None] == col_ids[None, :])
        ).astype(jnp.float32)
        to_slot = ((shard_of * slot_cap + same_rank)[:, None] == dest_ids[None, :]).astype(
            jnp.float32
        )
        select = jnp.dot(to_column.T, to_slot).astype(jnp.bfloat16)
        chosen = jnp.einsum("kj,jbw->kbw", select, incoming, preferred_element_type=jnp.float32)
        chosen = chosen.astype(jnp.bfloat16).reshape(col_blocks * BS, panel_width)
        place = ((chosen_pos[:, None] == local_pos[None, :]) & is_valid[:, None]).astype(
            jnp.bfloat16
        )
        left_local = jnp.einsum(
            "kj,jbw->kbw", place, local_blocks, preferred_element_type=jnp.float32
        )
        left_local = left_local.reshape(max_rows * BS, panel_width)

        def partial_rows(first_row, row_count, picked=picked, chosen=chosen):
            return jnp.dot(picked, chosen, preferred_element_type=jnp.float32)

        mine_sums = lax.psum_scatter(
            partial_rows(jnp.int32(0), own_rows * lax.axis_size("col")),
            "col",
            scatter_dimension=0,
            tiled=True,
        )
        own_left = sent_and_summed(left_local.astype(jnp.bfloat16), "col", 0).astype(jnp.bfloat16)
        contrib = exact_product(own_left, mine_sums)
        panel_sums.append(mine_sums)
        diag_terms.append(contrib)
    diag_total = lax.psum(jnp.stack(diag_terms), ("row", "col"))
    return (jnp.stack(panel_sums), -diag_total)


def solution(mesh):
    return jax.shard_map(
        local,
        mesh=mesh,
        in_specs=(P("row", "col"), P(None, "col", None), P(), P()),
        out_specs=(P(None, ("row", "col"), None), P()),
        check_vma=False,
    )
```

profile of v0, /device:TPU:1, one launch (start us, length us, event | category | flops | bytes accessed | tf_op | source)
XLA Modules:
  0.0 414.8 jit_solution(4478664436259446148)
XLA Ops:
  8.1 1.3 fusion.60
  11.7 2.5 copy.41
  14.2 9.3 %all-to-all-start.1 = ((bf16[16,128,512]{2,1,0:T(8,128)(2,1)}), bf16[16,128,512]{2,1,0:T(8,128)(2,1)S(1)}, u32[]{:S(2)}, u32[]{:S(2)}) async-start(bf16[16,128,512]{2,1,0:T(8,128)(2,1)} %copy.41), calls=%async_computation.2 | async-start | bytes 4194304 | tf_op jit(solution)/shard_map/all_to_all | solution.py:82
  23.6 2.0 sort.32
  27.0 8.2 %gather_fusion.7 = bf16[16,128,1664]{2,1,0:T(8,128)(2,1)} fusion(bf16[26,128,1664]{2,1,0:T(8,128)(2,1)} %bitcast.73, s32[1024]{0:T(1024)S(1)} %pad_clamp_fusion), kind=kCustom, calls=%fused_computation.7 | custom fusion | bytes 13631552 | tf_op jit(solution)/shard_map/gather | solution.py:63
  35.2 6.4 %broadcast_select_fusion = bf16[16,128,1664]{2,1,0:T(8,128)(2,1)} fusion(bf16[16,128,1664]{2,1,0:T(8,128)(2,1)} %gather_fusion.7, pred[16]{0:T(512)(128)(4,1)S(1)} %gather_fusion.5), kind=kLoop, calls=%fused_computation.10 | loop fusion | flops 3407872 | bytes 13631504 | tf_op jit(solution)/shard_map/jit(_where)/select_n | solution.py:64
  41.6 10.4 %all-to-all-done.1 = bf16[16,128,512]{2,1,0:T(8,128)(2,1)S(1)} async-done(((bf16[16,128,512]{2,1,0:T(8,128)(2,1)}), bf16[16,128,512]{2,1,0:T(8,128)(2,1)S(1)}, u32[]{:S(2)}, u32[]{:S(2)}) %all-to-all-start.1) | async-done | bytes 2097184 | tf_op jit(solution)/shard_map/all_to_all | solution.py:82
  52.0 2.8 fusion.7
  54.8 2.6 copy.43
  57.4 8.6 %fusion.64 = f32[2048,512]{1,0:T(8,128)} fusion(bf16[2048,1664]{1,0:T(8,128)(2,1)} %bitcast.76, bf16[1664,512]{1,0:T(8,128)(2,1)S(1)} %bitcast.81), kind=kOutput, calls=%fused_computation.117 | convolution fusion | flops 3489660928 | bytes 12713984 | tf_op jit(solution)/shard_map/dot_general | solution.py:103
  68.2 2.5 copy.37
  70.7 7.1 %all-to-all-start = ((bf16[16,128,512]{2,1,0:T(8,128)(2,1)}), bf16[16,128,512]{2,1,0:T(8,128)(2,1)S(1)}, u32[]{:S(2)}, u32[]{:S(2)}) async-start(bf16[16,128,512]{2,1,0:T(8,128)(2,1)} %copy.37), calls=%async_computation | async-start | bytes 4194304 | tf_op jit(solution)/shard_map/all_to_all | solution.py:82
  78.0 2.0 sort.31
  80.8 8.8 %gather_fusion.2 = bf16[16,128,1664]{2,1,0:T(8,128)(2,1)} fusion(bf16[26,128,1664]{2,1,0:T(8,128)(2,1)} %bitcast.74, s32[1024]{0:T(1024)S(1)} %pad_clamp_fusion.3), kind=kCustom, calls=%fused_computation.2 | custom fusion | bytes 13631552 | tf_op jit(solution)/shard_map/gather | solution.py:63
  90.2 6.4 %broadcast_select_fusion.1 = bf16[16,128,1664]{2,1,0:T(8,128)(2,1)} fusion(bf16[16,128,1664]{2,1,0:T(8,128)(2,1)} %gather_fusion.2, pred[16]{0:T(512)(128)(4,1)S(1)} %gather_fusion), kind=kLoop, calls=%fused_computation.11 | loop fusion | flops 3407872 | bytes 13631504 | tf_op jit(solution)/shard_map/jit(_where)/select_n | solution.py:64
  96.6 9.7 %all-to-all-done = bf16[16,128,512]{2,1,0:T(8,128)(2,1)S(1)} async-done(((bf16[16,128,512]{2,1,0:T(8,128)(2,1)}), bf16[16,128,512]{2,1,0:T(8,128)(2,1)S(1)}, u32[]{:S(2)}, u32[]{:S(2)}) %all-to-all-start) | async-done | bytes 2097184 | tf_op jit(solution)/shard_map/all_to_all | solution.py:82
  106.3 2.8 fusion.4
  109.1 2.6 copy.39
  111.7 8.5 %fusion.63 = f32[2048,512]{1,0:T(8,128)} fusion(bf16[2048,1664]{1,0:T(8,128)(2,1)} %bitcast.75, bf16[1664,512]{1,0:T(8,128)(2,1)S(1)} %bitcast.82), kind=kOutput, calls=%fused_computation.116 | convolution fusion | flops 3489660928 | bytes 12713984 | tf_op jit(solution)/shard_map/dot_general | solution.py:103
  121.2 2.5 copy.47
  123.7 10.4 %all-to-all-start.3 = ((bf16[16,128,512]{2,1,0:T(8,128)(2,1)}), bf16[16,128,512]{2,1,0:T(8,128)(2,1)S(1)}, u32[]{:S(2)}, u32[]{:S(2)}) async-start(bf16[16,128,512]{2,1,0:T(8,128)(2,1)} %copy.47), calls=%async_computation.5 | async-start | bytes 4194304 | tf_op jit(solution)/shard_map/all_to_all | solution.py:17
  134.9 2.5 copy.45
  137.3 28.3 %all-to-all-done.3 = bf16[16,128,512]{2,1,0:T(8,128)(2,1)S(1)} async-done(((bf16[16,128,512]{2,1,0:T(8,128)(2,1)}), bf16[16,128,512]{2,1,0:T(8,128)(2,1)S(1)}, u32[]{:S(2)}, u32[]{:S(2)}) %all-to-all-start.3) | async-done | bytes 2097184 | tf_op jit(solution)/shard_map/all_to_all | solution.py:17
  165.7 7.6 %all-to-all-start.2 = ((bf16[16,128,512]{2,1,0:T(8,128)(2,1)}), bf16[16,128,512]{2,1,0:T(8,128)(2,1)}, u32[]{:S(2)}, u32[]{:S(2)}) async-start(bf16[16,128,512]{2,1,0:T(8,128)(2,1)} %copy.45), calls=%async_computation.4 | async-start | bytes 4194304 | tf_op jit(solution)/shard_map/all_to_all | solution.py:17
  173.8 28.0 %all-to-all-done.2 = bf16[16,128,512]{2,1,0:T(8,128)(2,1)} async-done(((bf16[16,128,512]{2,1,0:T(8,128)(2,1)}), bf16[16,128,512]{2,1,0:T(8,128)(2,1)}, u32[]{:S(2)}, u32[]{:S(2)}) %all-to-all-start.2) | async-done | bytes 2097184 | tf_op jit(solution)/shard_map/all_to_all | solution.py:17
  201.8 1.9 reduce_sum.54
  203.8 1.6 convolution_bitcast_fusion
  205.4 43.9 %reduce-scatter.3.cloned.1.call-done = f32[128,512]{1,0:T(8,128)} async-done(((f32[2048,512]{1,0:T(8,128)}), f32[128,512]{1,0:T(8,128)}) %reduce-scatter.3.cloned.1.call-update) | async-done | bytes 262160 | tf_op jit(solution)/shard_map/reduce_scatter | solution.py:105
  249.2 1.6 convolution_bitcast_fusion.1
  250.8 1.5 pad_maximum_fusion
  254.2 150.9 %all-reduce.2.cloned.1.call-done = f32[2,512,512]{2,1,0:T(8,128)} async-done(((f32[2,512,512]{2,1,0:T(8,128)}), f32[2,512,512]{2,1,0:T(8,128)}) %all-reduce.2.cloned.1.call-update) | async-done | bytes 2097168 | tf_op jit(solution)/shard_map/psum | solution.py:115
  405.1 3.1 neg.3
  (50 shorter events, 12.5 us)
Async XLA Ops:
  14.2 37.8 %all-to-all-start.1 = ((bf16[16,128,512]{2,1,0:T(8,128)(2,1)}), bf16[16,128,512]{2,1,0:T(8,128)(2,1)S(1)}, u32[]{:S(2)}, u32[]{:S(2)}) async-start(bf16[16,128,512]{2,1,0:T(8,128)(2,1)} %copy.41), calls=%async_computation.2 | async-start | bytes 4194304 | tf_op jit(solution)/shard_map/all_to_all | solution.py:82
  23.5 180.2 %reduce-scatter.5.cloned.1.call-start = ((), (), s32[]{:S(2)}) async-start(), calls=%async_computation.7 | async-start | bytes 4456448 | tf_op jit(solution)/shard_map/reduce_scatter | solution.py:105
  70.7 35.6 %all-to-all-start = ((bf16[16,128,512]{2,1,0:T(8,128)(2,1)}), bf16[16,128,512]{2,1,0:T(8,128)(2,1)S(1)}, u32[]{:S(2)}, u32[]{:S(2)}) async-start(bf16[16,128,512]{2,1,0:T(8,128)(2,1)} %copy.37), calls=%async_computation | async-start | bytes 4194304 | tf_op jit(solution)/shard_map/all_to_all | solution.py:82
  77.8 171.4 %reduce-scatter.3.cloned.1.call-start = ((), (), s32[]{:S(2)}) async-start(), calls=%async_computation.6 | async-start | bytes 4456448 | tf_op jit(solution)/shard_map/reduce_scatter | solution.py:105
  123.7 42.0 %all-to-all-start.3 = ((bf16[16,128,512]{2,1,0:T(8,128)(2,1)}), bf16[16,128,512]{2,1,0:T(8,128)(2,1)S(1)}, u32[]{:S(2)}, u32[]{:S(2)}) async-start(bf16[16,128,512]{2,1,0:T(8,128)(2,1)} %copy.47), calls=%async_computation.5 | async-start | bytes 4194304 | tf_op jit(solution)/shard_map/all_to_all | solution.py:17
  165.7 36.2 %all-to-all-start.2 = ((bf16[16,128,512]{2,1,0:T(8,128)(2,1)}), bf16[16,128,512]{2,1,0:T(8,128)(2,1)}, u32[]{:S(2)}, u32[]{:S(2)}) async-start(bf16[16,128,512]{2,1,0:T(8,128)(2,1)} %copy.45), calls=%async_computation.4 | async-start | bytes 4194304 | tf_op jit(solution)/shard_map/all_to_all | solution.py:17
  173.3 231.9 %all-reduce.2.cloned.1.call-start = ((), (), s32[]{:S(2)}) async-start(), calls=%async_computation.8 | async-start | bytes 4194304 | tf_op jit(solution)/shard_map/psum | solution.py:115
  252.3 0.9 copy-start
  252.3 1.0 copy-start.1
Sparse Core Ops, SparseCore 0:
  66.1 95.6 reduce-scatter.4
  166.4 82.7 reduce-scatter.2
  254.6 150.4 all-reduce.1
where the time goes:
time: 416 us; the launch traced here: 415 us
  waiting for transfers between devices  271 us (65%)
  local copies, waits for them, and re-layouts  39.6 us (10%)
  starting transfers between devices  34.9 us (8%)
  matrix products  29.4 us (7%)
  other arithmetic  25.7 us (6%)
  between operations  13.9 us (3%)
    psum x1, waiting for transfers between devices, local(): diag_total = lax.psum(jnp.stack(diag_terms), ('row', 'col'))  151 us
    all_to_all x2, waiting for transfers between devices, sent_and_summed(): lax.all_to_all(pieces, axis, split_axis=0, concat_axis=0, tiled=True)  56.3 us
    reduce_scatter x2, waiting for transfers between devices, local(): lax.psum_scatter(partial_rows(jnp.int32(0), own_rows * lax.axis_size('col...  43.9 us
    all_to_all x2, waiting for transfers between devices, local(): lax.all_to_all(outgoing, 'col', split_axis=0, concat_axis=0, tiled=True)  20.1 us
    gather x4, local copies, waits for them, and re-layouts, local(): picked = a_blocks[local_row[supernode][chosen_pos]]  18.3 us
    all_to_all x2, starting transfers between devices, sent_and_summed(): lax.all_to_all(pieces, axis, split_axis=0, concat_axis=0, tiled=True)  18 us
    dot_general x2, matrix products, partial_rows(): return jnp.dot(picked, chosen, preferred_element_type=jnp.float32)  17.1 us
    all_to_all x2, starting transfers between devices, local(): lax.all_to_all(outgoing, 'col', split_axis=0, concat_axis=0, tiled=True)  16.4 us
  transfers between devices with their start and end apart: 7, of which 6 were waited for; matrix products, arithmetic and copies ran while one was open for 16% of the time, Pallas kernels for 0%

commit v1 on v0

--- a/solution.py
+++ b/solution.py
@@ -112,7 +112,7 @@
         contrib = exact_product(own_left, mine_sums)
         panel_sums.append(mine_sums)
         diag_terms.append(contrib)
-    diag_total = lax.psum(jnp.stack(diag_terms), ("row", "col"))
+    diag_total = lax.psum(lax.psum(jnp.stack(diag_terms), "row"), "col")
     return (jnp.stack(panel_sums), -diag_total)
 
 

time: 416 us -> 492 us (1.18)
  waiting for transfers between devices: 271 us -> 348 us
    psum x1 -> x2, waiting for transfers between devices: 151 us -> 228 us  [local(): diag_total = lax.psum(lax.psum(jnp.stack(diag_terms), 'row'), 'col')]
  transfers between devices with their start and end apart: 7 -> 8, of which waited for: 6 -> 7; matrix products, arithmetic and copies ran while one was open for 16% -> 14% of each run, Pallas kernels for 0% -> 0%
where the time goes in v1:
time: 492 us; the launch traced here: 491 us
  waiting for transfers between devices  348 us (71%)
  local copies, waits for them, and re-layouts  38.6 us (8%)
  starting transfers between devices  34.9 us (7%)
  matrix products  29.4 us (6%)
  other arithmetic  25.7 us (5%)
  between operations  14 us (3%)
    psum x2, waiting for transfers between devices, local(): diag_total = lax.psum(lax.psum(jnp.stack(diag_terms), 'row'), 'col')  228 us
    all_to_all x2, waiting for transfers between devices, sent_and_summed(): lax.all_to_all(pieces, axis, split_axis=0, concat_axis=0, tiled=True)  56.3 us
    reduce_scatter x2, waiting for transfers between devices, local(): lax.psum_scatter(partial_rows(jnp.int32(0), own_rows * lax.axis_size('col...  43.9 us
    all_to_all x2, waiting for transfers between devices, local(): lax.all_to_all(outgoing, 'col', split_axis=0, concat_axis=0, tiled=True)  20.1 us
    gather x4, local copies, waits for them, and re-layouts, local(): picked = a_blocks[local_row[supernode][chosen_pos]]  18.3 us
    all_to_all x2, starting transfers between devices, sent_and_summed(): lax.all_to_all(pieces, axis, split_axis=0, concat_axis=0, tiled=True)  17.9 us
    dot_general x2, matrix products, partial_rows(): return jnp.dot(picked, chosen, preferred_element_type=jnp.float32)  17.1 us
    all_to_all x2, starting transfers between devices, local(): lax.all_to_all(outgoing, 'col', split_axis=0, concat_axis=0, tiled=True)  16.4 us
  transfers between devices with their start and end apart: 8, of which 7 were waited for; matrix products, arithmetic and copies ran while one was open for 14% of the time, Pallas kernels for 0%

profile of v1, /device:TPU:1, one launch (start us, length us, event | category | flops | bytes accessed | tf_op | source)
XLA Modules:
  0.0 490.9 jit_solution(12541726620302739668)
XLA Ops:
  11.7 2.5 copy.41
  14.2 9.3 %all-to-all-start.1 = ((bf16[16,128,512]{2,1,0:T(8,128)(2,1)}), bf16[16,128,512]{2,1,0:T(8,128)(2,1)S(1)}, u32[]{:S(2)}, u32[]{:S(2)}) async-start(bf16[16,128,512]{2,1,0:T(8,128)(2,1)} %copy.41), calls=%async_computation.2 | async-start | bytes 4194304 | tf_op jit(solution)/shard_map/all_to_all | solution.py:82
  23.6 2.0 sort.32
  27.0 8.2 %gather_fusion.7 = bf16[16,128,1664]{2,1,0:T(8,128)(2,1)} fusion(bf16[26,128,1664]{2,1,0:T(8,128)(2,1)} %bitcast.73, s32[1024]{0:T(1024)S(1)} %pad_clamp_fusion), kind=kCustom, calls=%fused_computation.7 | custom fusion | bytes 13631552 | tf_op jit(solution)/shard_map/gather | solution.py:63
  35.2 6.4 %broadcast_select_fusion = bf16[16,128,1664]{2,1,0:T(8,128)(2,1)} fusion(bf16[16,128,1664]{2,1,0:T(8,128)(2,1)} %gather_fusion.7, pred[16]{0:T(512)(128)(4,1)S(1)} %gather_fusion.5), kind=kLoop, calls=%fused_computation.10 | loop fusion | flops 3407872 | bytes 13631504 | tf_op jit(solution)/shard_map/jit(_where)/select_n | solution.py:64
  41.6 10.4 %all-to-all-done.1 = bf16[16,128,512]{2,1,0:T(8,128)(2,1)S(1)} async-done(((bf16[16,128,512]{2,1,0:T(8,128)(2,1)}), bf16[16,128,512]{2,1,0:T(8,128)(2,1)S(1)}, u32[]{:S(2)}, u32[]{:S(2)}) %all-to-all-start.1) | async-done | bytes 2097184 | tf_op jit(solution)/shard_map/all_to_all | solution.py:82
  52.0 2.8 fusion.7
  54.8 2.6 copy.43
  57.4 8.6 %fusion.64 = f32[2048,512]{1,0:T(8,128)} fusion(bf16[2048,1664]{1,0:T(8,128)(2,1)} %bitcast.76, bf16[1664,512]{1,0:T(8,128)(2,1)S(1)} %bitcast.81), kind=kOutput, calls=%fused_computation.117 | convolution fusion | flops 3489660928 | bytes 12713984 | tf_op jit(solution)/shard_map/dot_general | solution.py:103
  68.2 2.5 copy.37
  70.7 7.1 %all-to-all-start = ((bf16[16,128,512]{2,1,0:T(8,128)(2,1)}), bf16[16,128,512]{2,1,0:T(8,128)(2,1)S(1)}, u32[]{:S(2)}, u32[]{:S(2)}) async-start(bf16[16,128,512]{2,1,0:T(8,128)(2,1)} %copy.37), calls=%async_computation | async-start | bytes 4194304 | tf_op jit(solution)/shard_map/all_to_all | solution.py:82
  78.0 2.0 sort.31
  80.8 8.8 %gather_fusion.2 = bf16[16,128,1664]{2,1,0:T(8,128)(2,1)} fusion(bf16[26,128,1664]{2,1,0:T(8,128)(2,1)} %bitcast.74, s32[1024]{0:T(1024)S(1)} %pad_clamp_fusion.3), kind=kCustom, calls=%fused_computation.2 | custom fusion | bytes 13631552 | tf_op jit(solution)/shard_map/gather | solution.py:63
  90.2 6.4 %broadcast_select_fusion.1 = bf16[16,128,1664]{2,1,0:T(8,128)(2,1)} fusion(bf16[16,128,1664]{2,1,0:T(8,128)(2,1)} %gather_fusion.2, pred[16]{0:T(512)(128)(4,1)S(1)} %gather_fusion), kind=kLoop, calls=%fused_computation.11 | loop fusion | flops 3407872 | bytes 13631504 | tf_op jit(solution)/shard_map/jit(_where)/select_n | solution.py:64
  96.6 9.7 %all-to-all-done = bf16[16,128,512]{2,1,0:T(8,128)(2,1)S(1)} async-done(((bf16[16,128,512]{2,1,0:T(8,128)(2,1)}), bf16[16,128,512]{2,1,0:T(8,128)(2,1)S(1)}, u32[]{:S(2)}, u32[]{:S(2)}) %all-to-all-start) | async-done | bytes 2097184 | tf_op jit(solution)/shard_map/all_to_all | solution.py:82
  106.3 2.8 fusion.4
  109.1 2.6 copy.39
  111.7 8.5 %fusion.63 = f32[2048,512]{1,0:T(8,128)} fusion(bf16[2048,1664]{1,0:T(8,128)(2,1)} %bitcast.75, bf16[1664,512]{1,0:T(8,128)(2,1)S(1)} %bitcast.82), kind=kOutput, calls=%fused_computation.116 | convolution fusion | flops 3489660928 | bytes 12713984 | tf_op jit(solution)/shard_map/dot_general | solution.py:103
  121.2 2.5 copy.47
  123.7 10.4 %all-to-all-start.3 = ((bf16[16,128,512]{2,1,0:T(8,128)(2,1)}), bf16[16,128,512]{2,1,0:T(8,128)(2,1)S(1)}, u32[]{:S(2)}, u32[]{:S(2)}) async-start(bf16[16,128,512]{2,1,0:T(8,128)(2,1)} %copy.47), calls=%async_computation.5 | async-start | bytes 4194304 | tf_op jit(solution)/shard_map/all_to_all | solution.py:17
  134.9 2.5 copy.45
  137.4 28.3 %all-to-all-done.3 = bf16[16,128,512]{2,1,0:T(8,128)(2,1)S(1)} async-done(((bf16[16,128,512]{2,1,0:T(8,128)(2,1)}), bf16[16,128,512]{2,1,0:T(8,128)(2,1)S(1)}, u32[]{:S(2)}, u32[]{:S(2)}) %all-to-all-start.3) | async-done | bytes 2097184 | tf_op jit(solution)/shard_map/all_to_all | solution.py:17
  165.7 7.5 %all-to-all-start.2 = ((bf16[16,128,512]{2,1,0:T(8,128)(2,1)}), bf16[16,128,512]{2,1,0:T(8,128)(2,1)}, u32[]{:S(2)}, u32[]{:S(2)}) async-start(bf16[16,128,512]{2,1,0:T(8,128)(2,1)} %copy.45), calls=%async_computation.4 | async-start | bytes 4194304 | tf_op jit(solution)/shard_map/all_to_all | solution.py:17
  173.8 28.0 %all-to-all-done.2 = bf16[16,128,512]{2,1,0:T(8,128)(2,1)} async-done(((bf16[16,128,512]{2,1,0:T(8,128)(2,1)}), bf16[16,128,512]{2,1,0:T(8,128)(2,1)}, u32[]{:S(2)}, u32[]{:S(2)}) %all-to-all-start.2) | async-done | bytes 2097184 | tf_op jit(solution)/shard_map/all_to_all | solution.py:17
  201.8 1.9 reduce_sum.54
  203.7 1.6 convolution_bitcast_fusion
  205.3 43.8 %reduce-scatter.3.cloned.1.call-done = f32[128,512]{1,0:T(8,128)} async-done(((f32[2048,512]{1,0:T(8,128)}), f32[128,512]{1,0:T(8,128)}) %reduce-scatter.3.cloned.1.call-update) | async-done | bytes 262160 | tf_op jit(solution)/shard_map/reduce_scatter | solution.py:105
  249.2 1.6 convolution_bitcast_fusion.1
  250.7 1.5 pad_maximum_fusion
  252.4 78.6 %all-reduce.3.cloned.1.call-done = f32[2,512,512]{2,1,0:T(8,128)} async-done(((f32[2,512,512]{2,1,0:T(8,128)}), f32[2,512,512]{2,1,0:T(8,128)}) %all-reduce.3.cloned.1.call-update) | async-done | bytes 2097168 | tf_op jit(solution)/shard_map/psum | solution.py:115
  331.9 149.3 %all-reduce.5.cloned.1.call-done = f32[2,512,512]{2,1,0:T(8,128)} async-done(((f32[2,512,512]{2,1,0:T(8,128)}), f32[2,512,512]{2,1,0:T(8,128)}) %all-reduce.5.cloned.1.call-update) | async-done | bytes 2097168 | tf_op jit(solution)/shard_map/psum | solution.py:115
  481.2 3.1 neg.3
  (53 shorter events, 12.9 us)
Async XLA Ops:
  14.2 37.8 %all-to-all-start.1 = ((bf16[16,128,512]{2,1,0:T(8,128)(2,1)}), bf16[16,128,512]{2,1,0:T(8,128)(2,1)S(1)}, u32[]{:S(2)}, u32[]{:S(2)}) async-start(bf16[16,128,512]{2,1,0:T(8,128)(2,1)} %copy.41), calls=%async_computation.2 | async-start | bytes 4194304 | tf_op jit(solution)/shard_map/all_to_all | solution.py:82
  23.5 180.2 %reduce-scatter.5.cloned.1.call-start = ((), (), s32[]{:S(2)}) async-start(), calls=%async_computation.7 | async-start | bytes 4456448 | tf_op jit(solution)/shard_map/reduce_scatter | solution.py:105
  70.7 35.6 %all-to-all-start = ((bf16[16,128,512]{2,1,0:T(8,128)(2,1)}), bf16[16,128,512]{2,1,0:T(8,128)(2,1)S(1)}, u32[]{:S(2)}, u32[]{:S(2)}) async-start(bf16[16,128,512]{2,1,0:T(8,128)(2,1)} %copy.37), calls=%async_computation | async-start | bytes 4194304 | tf_op jit(solution)/shard_map/all_to_all | solution.py:82
  77.8 171.4 %reduce-scatter.3.cloned.1.call-start = ((), (), s32[]{:S(2)}) async-start(), calls=%async_computation.6 | async-start | bytes 4456448 | tf_op jit(solution)/shard_map/reduce_scatter | solution.py:105
  123.7 42.0 %all-to-all-start.3 = ((bf16[16,128,512]{2,1,0:T(8,128)(2,1)}), bf16[16,128,512]{2,1,0:T(8,128)(2,1)S(1)}, u32[]{:S(2)}, u32[]{:S(2)}) async-start(bf16[16,128,512]{2,1,0:T(8,128)(2,1)} %copy.47), calls=%async_computation.5 | async-start | bytes 4194304 | tf_op jit(solution)/shard_map/all_to_all | solution.py:17
  165.7 36.1 %all-to-all-start.2 = ((bf16[16,128,512]{2,1,0:T(8,128)(2,1)}), bf16[16,128,512]{2,1,0:T(8,128)(2,1)}, u32[]{:S(2)}, u32[]{:S(2)}) async-start(bf16[16,128,512]{2,1,0:T(8,128)(2,1)} %copy.45), calls=%async_computation.4 | async-start | bytes 4194304 | tf_op jit(solution)/shard_map/all_to_all | solution.py:17
  173.2 157.8 %all-reduce.3.cloned.1.call-start = ((), (), s32[]{:S(2)}) async-start(), calls=%async_computation.8 | async-start | bytes 4194304 | tf_op jit(solution)/shard_map/psum | solution.py:115
  252.3 78.8 %copy-start = (f32[128,512]{1,0:T(8,128)S(1)}, f32[128,512]{1,0:T(8,128)}, u32[]{:S(2)}) copy-start(f32[128,512]{1,0:T(8,128)} %reduce-scatter.5.cloned.1.call-done) | copy-start | bytes 786436
  252.3 78.8 %copy-start.1 = (f32[128,512]{1,0:T(8,128)S(1)}, f32[128,512]{1,0:T(8,128)}, u32[]{:S(2)}) copy-start(f32[128,512]{1,0:T(8,128)} %reduce-scatter.3.cloned.1.call-done) | copy-start | bytes 786436
  252.3 228.9 %all-reduce.5.cloned.1.call-start = ((), (), s32[]{:S(2)}) async-start(), calls=%async_computation.9 | async-start | bytes 4194304 | tf_op jit(solution)/shard_map/psum | solution.py:115
Sparse Core Ops, SparseCore 0:
  66.1 95.5 reduce-scatter.4
  166.3 82.8 reduce-scatter.2
  252.4 78.5 all-reduce.2
  333.4 147.7 all-reduce.4
